TPU v7x, 256 devices: a whole 4x4x8 slice. The times are simulated.
256 devices in a mesh: dp: 8 (over y_hi, x), mp: 32 (over z, y_lo, core).
Axes of the slice: x: 4, y: 4 (y_hi: 2, y_lo: 2; y = y_hi * 2 + y_lo), z: 8, core: 2. Of those that a mesh axis runs over, the one named last changes fastest.
Arguments:
- tokens: bfloat16 [2048, 6144], P('dp', 'mp'), may hold values from -15 to 15
- upstream: bfloat16 [2048, 6144], P('dp', 'mp'), may hold values from -6.4 to 6.4
- norm_gain: float32 [6144], replicated, may hold values from 0.1 to 1.9
- w_in: bfloat16 [6144, 12288], P(None, 'mp'), may hold values from -0.08930431 to 0.08930431
- w_out: bfloat16 [12288, 6144], P('mp'), may hold values from -0.0550287 to 0.0550287
Outputs:
- output: bfloat16 [2048, 6144], P('dp', 'mp')
- grad_tokens: bfloat16 [2048, 6144], P('dp', 'mp')
- grad_in: float32 [6144, 12288], P('dp', 'mp')
- grad_out: float32 [12288, 6144], P('mp', 'dp')
All inputs are finite; a program needn't handle non-finite values.
Results may differ from a plain program's by a relative error of at most 0.019.
Values may be sent and summed in bfloat16 or wider, within the bound.
A program may use at most 128 MiB of HBM per device.

v0:
```python
import jax
import jax.numpy as jnp
from jax import lax
from jax.sharding import PartitionSpec as P

D = 6144


def gelu_slope(value):
    cumul = 0.5 * (1.0 + lax.erf(value * 0.7071067811865476))
    dense = jnp.exp(-0.5 * value * value) * 0.3989422804014327
    return cumul + value * dense


def body(tokens, upstream, norm_gain, w_in, w_out):
    feat_width = tokens.shape[1]
    feat_start = lax.axis_index("mp") * feat_width
    gain_local = lax.dynamic_slice_in_dim(norm_gain, feat_start, feat_width, 0)
    tokens_f = tokens.astype(jnp.float32)
    row_total = lax.psum(jnp.sum(tokens_f, axis=1, keepdims=True), "mp")
    mean_row = row_total / D
    centred = tokens_f - mean_row
    spread = lax.psum(jnp.sum(centred * centred, axis=1, keepdims=True), "mp")
    inv_std = lax.rsqrt(spread / D + 1e-06)
    unit_rows = centred * inv_std
    normed = (unit_rows * gain_local[None, :]).astype(jnp.bfloat16)
    piece = lax.all_gather(normed, "mp", axis=1, tiled=True)
    w_part = w_in
    total = jnp.dot(piece, w_part, preferred_element_type=jnp.float32)
    filled = piece
    preact = total
    normed_all = filled
    hidden = jax.nn.gelu(preact, approximate=False).astype(jnp.bfloat16)
    w_part = w_out
    branch = (
        lax.psum_scatter(
            lax.dot_general(
                w_part, hidden, (((0,), (1,)), ((), ())), preferred_element_type=jnp.float32
            ).astype(jnp.bfloat16),
            "mp",
            scatter_dimension=0,
            tiled=True,
        )
        .astype(jnp.float32)
        .T
    )
    output = (tokens_f + branch).astype(jnp.bfloat16)
    piece = lax.all_gather(upstream, "mp", axis=1, tiled=True)
    w_part = w_out
    total = lax.dot_general(
        piece, w_part, (((1,), (1,)), ((), ())), preferred_element_type=jnp.float32
    )
    filled = piece
    grad_preact = (total * gelu_slope(preact)).astype(jnp.bfloat16)
    w_part = w_in
    grad_normed = (
        lax.psum_scatter(
            lax.dot_general(
                w_part, grad_preact, (((1,), (1,)), ((), ())), preferred_element_type=jnp.float32
            ).astype(jnp.bfloat16),
            "mp",
            scatter_dimension=0,
            tiled=True,
        )
        .astype(jnp.float32)
        .T
    )
    scaled = grad_normed * gain_local[None, :]
    scaled_sum, inner_sum = lax.psum(
        (
            jnp.sum(scaled, axis=1, keepdims=True),
            jnp.sum(scaled * unit_rows, axis=1, keepdims=True),
        ),
        "mp",
    )
    grad_ln = inv_std * (scaled - scaled_sum / D - unit_rows * (inner_sum / D))
    grad_tokens = (upstream.astype(jnp.float32) + grad_ln).astype(jnp.bfloat16)
    full_in = lax.dot_general(
        normed_all, grad_preact, (((0,), (0,)), ((), ())), preferred_element_type=jnp.float32
    )
    full_out = lax.dot_general(
        hidden, filled, (((0,), (0,)), ((), ())), preferred_element_type=jnp.float32
    )
    grad_in, grad_out = (
        lax.psum_scatter(
            full_in.astype(jnp.bfloat16), "dp", scatter_dimension=0, tiled=True
        ).astype(jnp.float32),
        lax.psum_scatter(
            full_out.astype(jnp.bfloat16), "dp", scatter_dimension=1, tiled=True
        ).astype(jnp.float32),
    )
    return (output, grad_tokens, grad_in, grad_out)


def solution(mesh):
    return jax.shard_map(
        body,
        mesh=mesh,
        in_specs=(P("dp", "mp"), P("dp", "mp"), P(), P(None, "mp"), P("mp", None)),
        out_specs=(P("dp", "mp"), P("dp", "mp"), P("dp", "mp"), P("mp", "dp")),
        check_vma=False,
    )
```

profile of v0, /device:TPU:10, one launch (start us, length us, event | category | flops | bytes accessed | tf_op | source)
XLA Modules:
  0.0 707.1 jit_solution(5920605068451340860)
XLA Ops:
  7.2 0.0 all-gather.3.cloned.1.call-start
  7.2 0.9 convert_reduce_fusion
  8.1 55.4 %psum.28 = f32[256,1]{0,1:T(1,128)S(1)} all-reduce(f32[256,1]{0,1:T(1,128)S(1)} %bitcast.40), channel_id=1, replica_groups=mesh['dp'=8,'mp'=32] {'mp'}, use_global_device_ids=true, to_apply=%region_1.0 | all-reduce | flops 256 | bytes 2048 | tf_op jit(solution)/shard_map/psum | solution.py:20
  63.5 0.9 fusion.28
  64.5 53.0 %psum.29 = f32[256,1]{0,1:T(1,128)S(1)} all-reduce(f32[256,1]{0,1:T(1,128)S(1)} %bitcast.41), channel_id=1, replica_groups=mesh['dp'=8,'mp'=32] {'mp'}, use_global_device_ids=true, to_apply=%region_3.0 | all-reduce | flops 256 | bytes 2048 | tf_op jit(solution)/shard_map/psum | solution.py:23
  117.4 0.8 dynamic_slice.3
  118.2 1.6 fusion.22
  119.8 0.0 all-gather.3.cloned.1.call-update
  119.9 0.0 all-gather.5.cloned.1.call-start
  119.9 0.7 all-gather.5.cloned.1.call-update
  120.6 0.0 reduce-scatter.15.cloned.1.call-start
  120.7 65.9 %all-gather.3.cloned.1.call-done = bf16[256,6144]{0,1:T(8,128)(2,1)} async-done(((bf16[256,192]{0,1:T(8,128)(2,1)}), bf16[256,6144]{0,1:T(8,128)(2,1)}) %all-gather.3.cloned.1.call-update) | async-done | bytes 3145744 | tf_op jit(solution)/shard_map/all_gather | solution.py:27
  186.5 5.1 fusion.33
  191.7 0.0 copy-start.4
  191.7 62.5 %all-gather.5.cloned.1.call-done = bf16[256,6144]{0,1:T(8,128)(2,1)} async-done(((bf16[256,192]{0,1:T(8,128)(2,1)}), bf16[256,6144]{0,1:T(8,128)(2,1)}) %all-gather.5.cloned.1.call-update) | async-done | bytes 3145744 | tf_op jit(solution)/shard_map/all_gather | solution.py:48
  254.1 0.0 copy-done.4
  254.2 0.0 copy-start
  254.2 5.3 fusion.2
  259.5 0.0 copy-done
  259.5 1.9 fusion.1
  261.4 2.8 copy.21
  264.2 0.0 reduce-scatter.15.cloned.1.call-update
  264.2 0.0 reduce-scatter.13.cloned.1.call-start
  264.3 5.0 fusion
  269.3 2.8 copy.19
  272.1 0.0 reduce-scatter.13.cloned.1.call-update
  272.1 0.0 reduce-scatter.11.cloned.1.call-start
  272.2 6.4 convolution_convert_fusion
  278.6 0.0 copy-start.1
  278.6 0.0 reduce-scatter.11.cloned.1.call-update
  278.6 0.2 reduce-scatter.9.cloned.1.call-start
  278.8 1.6 copy-done.1
  280.4 4.0 convolution_convert_fusion.1
  284.4 0.0 copy-start.2
  284.4 0.0 copy-start.3
  284.4 0.0 reduce-scatter.9.cloned.1.call-update
  284.4 97.0 %reduce-scatter.15.cloned.1.call-done = bf16[192,256]{1,0:T(8,128)(2,1)} async-done(((bf16[6144,256]{1,0:T(8,128)(2,1)}), bf16[192,256]{1,0:T(8,128)(2,1)}) %reduce-scatter.15.cloned.1.call-update) | async-done | bytes 98320 | tf_op jit(solution)/shard_map/reduce_scatter | solution.py:57
  381.4 1.0 fusion.30
  382.4 0.0 copy-done.2
  382.4 1.0 fusion.23
  383.4 53.6 %all-reduce = (f32[256,1]{0,1:T(1,128)S(1)}, f32[256,1]{0,1:T(1,128)S(1)}) all-reduce(f32[256,1]{0,1:T(1,128)S(1)} %bitcast.39, f32[256,1]{0,1:T(1,128)S(1)} %bitcast.38), channel_id=1, replica_groups=mesh['dp'=8,'mp'=32] {'mp'}, use_global_device_ids=true, to_apply=%region_9.0 | all-reduce | flops 512 | bytes 4096 | tf_op jit(solution)/shard_map/psum | solution.py:69
  437.1 65.7 %reduce-scatter.13.cloned.1.call-done = bf16[192,256]{1,0:T(8,128)(2,1)} async-done(((bf16[6144,256]{1,0:T(8,128)(2,1)}), bf16[192,256]{1,0:T(8,128)(2,1)}) %reduce-scatter.13.cloned.1.call-update) | async-done | bytes 98320 | tf_op jit(solution)/shard_map/reduce_scatter | solution.py:36
  502.8 0.0 copy-done.3
  502.8 1.7 fusion.27
  504.5 96.6 %reduce-scatter.11.cloned.1.call-done = bf16[384,768]{1,0:T(8,128)(2,1)} async-done(((bf16[384,6144]{1,0:T(8,128)(2,1)}), bf16[384,768]{1,0:T(8,128)(2,1)}) %reduce-scatter.11.cloned.1.call-update) | async-done | bytes 589840 | tf_op jit(solution)/shard_map/reduce_scatter | solution.py:88
  601.1 2.2 convert_element_type.64
  603.3 94.8 %reduce-scatter.9.cloned.1.call-done = bf16[768,384]{1,0:T(8,128)(2,1)} async-done(((bf16[6144,384]{1,0:T(8,128)(2,1)}), bf16[768,384]{1,0:T(8,128)(2,1)}) %reduce-scatter.9.cloned.1.call-update) | async-done | bytes 589840 | tf_op jit(solution)/shard_map/reduce_scatter | solution.py:85
  698.1 2.2 convert_element_type.62
  (3 shorter events, 0.0 us)
Async XLA Ops:
  7.2 179.4 %all-gather.3.cloned.1.call-start = ((), (), s32[]{:S(2)}) async-start(), calls=%async_computation.4 | async-start | bytes 3244032 | tf_op jit(solution)/shard_map/all_gather | solution.py:27
  119.9 134.3 %all-gather.5.cloned.1.call-start = ((), (), s32[]{:S(2)}) async-start(), calls=%async_computation.5 | async-start | bytes 3244032 | tf_op jit(solution)/shard_map/all_gather | solution.py:48
  120.6 260.8 %reduce-scatter.15.cloned.1.call-start = ((), (), s32[]{:S(2)}) async-start(), calls=%async_computation.9 | async-start | bytes 3244032 | tf_op jit(solution)/shard_map/reduce_scatter | solution.py:57
  191.7 62.5 %copy-start.4 = (f32[256,384]{1,0:T(8,128)}, f32[256,384]{1,0:T(8,128)S(1)}, u32[]{:S(2)}) copy-start(f32[256,384]{1,0:T(8,128)S(1)} %fusion.33) | copy-start | bytes 1179652
  254.2 5.3 copy-start
  264.2 238.6 %reduce-scatter.13.cloned.1.call-start = ((), (), s32[]{:S(2)}) async-start(), calls=%async_computation.8 | async-start | bytes 3244032 | tf_op jit(solution)/shard_map/reduce_scatter | solution.py:36
  272.1 329.0 %reduce-scatter.11.cloned.1.call-start = ((), (), s32[]{:S(2)}) async-start(), calls=%async_computation.7 | async-start | bytes 5308416 | tf_op jit(solution)/shard_map/reduce_scatter | solution.py:88
  278.6 1.9 copy-start.1
  278.6 419.5 %reduce-scatter.9.cloned.1.call-start = ((), (), s32[]{:S(2)}) async-start(), calls=%async_computation.6 | async-start | bytes 5308416 | tf_op jit(solution)/shard_map/reduce_scatter | solution.py:85
  284.4 98.0 %copy-start.2 = (bf16[256,192]{0,1:T(8,128)(2,1)S(1)}, bf16[256,192]{0,1:T(8,128)(2,1)}, u32[]{:S(2)}) copy-start(bf16[256,192]{0,1:T(8,128)(2,1)} %param.5) | copy-start | bytes 294916
  284.4 218.4 %copy-start.3 = (bf16[256,192]{0,1:T(8,128)(2,1)S(1)}, bf16[256,192]{0,1:T(8,128)(2,1)}, u32[]{:S(2)}) copy-start(bf16[256,192]{0,1:T(8,128)(2,1)} %param.6) | copy-start | bytes 294916
Sparse Core Ops, SparseCore 0:
  120.0 66.5 all-gather.2
  188.4 65.7 all-gather.4
  264.3 117.0 reduce-scatter.14
  384.0 118.7 reduce-scatter.12
  506.9 94.1 reduce-scatter.10
  605.8 92.2 reduce-scatter.8
where the time goes:
time: 709 us; the launch traced here: 707 us
  waiting for transfers between devices  483 us (68%)
  blocking collectives  162 us (23%)
  matrix products  27.7 us (4%)
  between operations  14.2 us (2%)
  other arithmetic  11.5 us (2%)
  local copies, waits for them, and re-layouts  8.08 us (1%)
    reduce_scatter x1, waiting for transfers between devices, body(): lax.psum_scatter(lax.dot_general(w_part, grad_preact, (((1,), (1,)), ((),...  97 us
    reduce_scatter x1, waiting for transfers between devices, body(): lax.psum_scatter(full_out.astype(jnp.bfloat16), 'dp', scatter_dimension=1...  96.6 us
    reduce_scatter x1, waiting for transfers between devices, body(): lax.psum_scatter(full_in.astype(jnp.bfloat16), 'dp', scatter_dimension=0,...  94.8 us
    all_gather x1, waiting for transfers between devices, body(): piece = lax.all_gather(normed, 'mp', axis=1, tiled=True)  65.9 us
    reduce_scatter x1, waiting for transfers between devices, body(): lax.psum_scatter(lax.dot_general(w_part, hidden, (((0,), (1,)), ((), ()))...  65.7 us
    all_gather x1, waiting for transfers between devices, body(): piece = lax.all_gather(upstream, 'mp', axis=1, tiled=True)  62.5 us
    psum x1, blocking collectives, body(): row_total = lax.psum(jnp.sum(tokens_f, axis=1, keepdims=True), 'mp')  55.4 us
    psum x1, blocking collectives, body(): lax.psum((jnp.sum(scaled, axis=1, keepdims=True), jnp.sum(scaled * unit_r...  53.6 us
  transfers between devices with their start and end apart: 6, of which 6 were waited for; matrix products, arithmetic and copies ran while one was open for 4% of the time, Pallas kernels for 0%

commit v1 on v0

v1 whole, which is shorter than its diff:
```python
import functools

import jax
import jax.numpy as jnp
from jax import lax
from jax.experimental import pallas as pl
from jax.experimental.pallas import tpu as pltpu
from jax.sharding import PartitionSpec as P

MESH = pl.DeviceIdType.MESH
F32, BF16 = jnp.float32, jnp.bfloat16
D = 6144
BLK = 768
W = 192
TG = 256
FB = 384
ORDER = (0, 1, 3, 2)
LAG = 2


def gelu_parts(v):
    cumul = 0.5 * (1.0 + lax.erf(v * 0.7071067811865476))
    dense = jnp.exp(-0.5 * v * v) * 0.3989422804014327
    return cumul, dense


def split_rows(row):
    n = row.shape[1]
    hi = row.astype(BF16).astype(F32)
    mid = (row - hi).astype(BF16).astype(F32)
    low = row - hi - mid
    index = lax.broadcasted_iota(jnp.int32, (16, n), 0)
    spread = [jnp.broadcast_to(v, (16, n)) for v in (hi, mid, low)]
    zero = jnp.zeros((16, n), F32)
    out = jnp.where(
        index == 0, spread[0], jnp.where(index == 1, spread[1], jnp.where(index == 2, spread[2], zero))
    )
    return out.astype(BF16)


def column(row):
    return jnp.broadcast_to(row, (128, row.shape[1])).T


def dot(a, b):
    return jnp.dot(a, b, preferred_element_type=F32)


def dot_t(a, b):
    return lax.dot_general(a, b, (((1,), (1,)), ((), ())), preferred_element_type=F32)


def kernel(
    x_ref, u_ref, gain_ref, w_in_ref, w_out_ref,
    out_ref, gt_ref, gi_ref, go_ref,
    xt, nt, wi, wit, wo, wot, gcol, gzcol, srow,
    st, mean_s, inv_s, ps, pr, po, pre, hg,
    bp, br, rz, acc, fin, smo, smc, smy, smz, gs, gr, gso, gro,
    loc_sem, org_s, ag_r, ag_z, sib_s, sib_r, st_s, st_r, p_s, p_r, hg_s, hg_r,
    b_s, b_r, rz_s, rz_r, fin_s, fin_r, sm_s, sm_r, smz_s, smz_r, gr_s, gr_r,
):
    dp, mp = lax.axis_index("dp"), lax.axis_index("mp")
    h, q = lax.div(dp, 4), lax.rem(dp, 4)
    z, yl, c = lax.div(mp, 4), lax.rem(lax.div(mp, 2), 2), lax.rem(mp, 2)

    def dev(h_, x_, z_, y_, c_):
        return (h_ * 4 + x_, z_ * 4 + y_ * 2 + c_)

    def xo(k):
        return lax.rem(q + k, 4)

    def zo(k):
        return lax.rem(z + k, 8)

    sibling = dev(h, q, z, yl, 1 - c)
    ypart = dev(h, q, z, 1 - yl, c)
    hpart = dev(1 - h, q, z, yl, c)
    zplus, zminus = dev(h, q, zo(1), yl, c), dev(h, q, zo(7), yl, c)

    def remote(src, dst, ss, rs, to):
        return pltpu.make_async_remote_copy(
            src_ref=src, dst_ref=dst, send_sem=ss, recv_sem=rs, device_id=to, device_id_type=MESH
        )

    def wi_copy(k):
        return pltpu.make_async_copy(w_in_ref.at[pl.ds(k * BLK, BLK)], wi.at[k], loc_sem.at[k])

    def wo_copy(b):
        start = pl.multiple_of((q + 4 * b) * BLK, BLK)
        return pltpu.make_async_copy(w_out_ref.at[:, pl.ds(start, BLK)], wo.at[b], loc_sem.at[8 + b])

    for k in range(8):
        wi_copy(k).start()
    for b in range(2):
        wo_copy(b).start()

    partners = [sibling, ypart, hpart]
    partners += [dev(h, q, zo(k), yl, c) for k in range(1, 8)]
    partners += [dev(h, xo(k), z, y_, c) for k in range(1, 4) for y_ in (yl, 1 - yl)]
    barrier = pltpu.get_barrier_semaphore()
    for p in partners:
        pl.semaphore_signal(barrier, inc=1, device_id=p, device_id_type=MESH)
    pl.semaphore_wait(barrier, len(partners))

    def rows(y2, cc):
        return pl.ds(pl.multiple_of(y2 * 384 + cc * W, 64), W)

    xs = lax.rem(z, 4)
    zb = lax.div(z, 4)
    mine = (x_ref, u_ref)

    def origin(arr, other):
        to = dev(h, xs, z, 1 - yl if other else yl, c)
        return remote(
            mine[arr], xt.at[arr, q, zb, rows(yl, c)], org_s.at[arr, other], ag_r.at[arr, q, zb, yl], to
        )

    for arr in range(2):

        @pl.when(xs != q)
        def _():
            origin(arr, 0).start()

        origin(arr, 1).start()

    @pl.when(xs == q)
    def _():
        for arr in range(2):
            xt[arr, q, zb, rows(yl, c), :] = mine[arr][...]

    def group(gi):
        if isinstance(gi, int):
            return lax.rem(q + ORDER[gi], 4)
        return lax.rem(q + gi + jnp.where(gi == 2, 1, 0) - jnp.where(gi == 3, 1, 0), 4)

    def place(b):
        rb = lax.rem(z - q + 8 - 4 * b, 8)
        return rb, jnp.minimum(rb, 8 - rb)

    def ag_item(n):
        arr, gi, y2 = lax.div(n, 8), lax.rem(lax.div(n, 2), 4), lax.rem(n, 2)
        return arr, group(gi), y2

    def ag_copies(b, rb, n):
        arr, g, y2 = ag_item(n)
        piece = xt.at[arr, g, b, rows(y2, c)]
        recv = ag_r.at[arr, g, b, y2]
        up = (rb <= 2) | ((rb == 3) & (y2 == 0))
        down = (rb == 0) | (rb >= 6) | ((rb == 5) & (y2 == 1))
        local = (rb == 0) & (g == q) & (y2 == yl)
        c_up = remote(piece, piece, ag_z.at[arr, g, b, y2, 0], recv, zplus)
        c_down = remote(piece, piece, ag_z.at[arr, g, b, y2, 1], recv, zminus)
        c_sib = remote(piece, piece, sib_s.at[arr, g, b, y2], sib_r.at[arr, g, b, y2], sibling)
        return up, down, local, c_up, c_down, c_sib

    def ag_step(s, _):
        for b in range(2):
            rb, dist = place(b)
            n = s - LAG * dist

            @pl.when((n >= 0) & (n < 16))
            def _():
                up, down, local, c_up, c_down, c_sib = ag_copies(b, rb, n)

                @pl.when(jnp.logical_not(local))
                def _():
                    c_up.wait_recv()

                pl.when(up)(c_up.start)
                pl.when(down)(c_down.start)
                c_sib.start()

        return 0

    def ag_steps(lo, hi):
        lax.fori_loop(lo, hi, ag_step, 0)

    def prep_wi(b):
        for k in range(4 * b, 4 * b + 4):
            wi_copy(k).wait()

    def prep_s(lo, hi):
        for k in range(lo, hi):
            term = dot(split_rows(gain_ref[k : k + 1, :]), wi[k])
            if k == 0:
                srow[...] = term
            else:
                srow[...] += term

    def prep_wit(b):
        for t in range(2):
            part = wi[q + 4 * b, pl.ds(t * 384, 384), :]
            wit[b, :, t * 384 : (t + 1) * 384] = part.T

    def prep_wot(b):
        wo_copy(b).wait()
        for t in range(2):
            wot[b, t * 384 : (t + 1) * 384, :] = wo[b, :, t * 384 : (t + 1) * 384].T

    def prep_gain():
        for b in range(2):
            gcol[b] = column(gain_ref[pl.ds(q + 4 * b, 1), :])
        gzcol[...] = column(gain_ref[pl.ds(z, 1), :])

    ag_steps(0, 1)
    prep_wi(0)
    prep_wi(1)
    ag_steps(1, 2)
    prep_gain()
    ag_steps(2, 3)
    prep_wit(0)
    ag_steps(3, 4)
    prep_wit(1)
    ag_steps(4, 5)
    prep_wot(0)
    ag_steps(5, 6)
    prep_wot(1)
    ag_steps(6, 7)
    prep_s(0, 3)
    ag_steps(7, 8)
    prep_s(3, 6)
    ag_steps(8, 9)
    prep_s(6, 8)

    def wait_sib(arr, g):
        for b in range(2):
            for y2 in range(2):
                piece = xt.at[arr, g, b, rows(y2, 1 - c)]
                remote(piece, piece, sib_s.at[arr, g, b, y2], sib_r.at[arr, g, b, y2], sibling).wait_recv()

    def st_copy(g, k):
        return remote(st.at[q, g], st.at[q, g], st_s.at[g, k], st_r.at[g, q], dev(h, xo(k), z, yl, c))

    def stats(gi):
        g = group(gi)
        wait_sib(0, g)

        def total(i, t):
            piece = xt[0, g, lax.div(i, 4), pl.ds(pl.multiple_of(lax.rem(i, 4) * W, 64), W), :]
            return t + jnp.sum(piece.astype(F32).reshape(W // 8, 8, TG), axis=0)

        t = lax.fori_loop(0, 8, total, jnp.zeros((8, TG), F32))
        mean = jnp.broadcast_to(jnp.sum(t, axis=0, keepdims=True) * (1.0 / (2 * BLK)), (8, TG))

        def square(i, t):
            piece = xt[0, g, lax.div(i, 4), pl.ds(pl.multiple_of(lax.rem(i, 4) * W, 64), W), :]
            d = piece.astype(F32).reshape(W // 8, 8, TG) - mean[None]
            return t + jnp.sum(d * d, axis=0)

        t = lax.fori_loop(0, 8, square, jnp.zeros((8, TG), F32))
        st[q, g, 0] = mean
        st[q, g, 1] = jnp.broadcast_to(jnp.sum(t, axis=0, keepdims=True), (8, TG))
        for k in range(1, 4):
            st_copy(g, k).start()

    def p_copy(arr, gi):
        g = group(gi)
        return remote(ps.at[arr, g], pr.at[arr, q], p_s.at[arr, g], p_r.at[arr, q], dev(h, g, z, yl, c))

    def put_part(arr, gi, part):
        if gi == 0:
            po[arr] = part
        else:
            ps[arr, group(gi)] = part.astype(BF16)
            p_copy(arr, gi).start()

    def norm_part(gi):
        g = group(gi)
        for k in range(1, 4):
            other = st.at[xo(k), g]
            remote(other, other, st_s.at[g, k], st_r.at[g, xo(k)], sibling).wait_recv()
        means = [st[i, g, 0] for i in range(4)]
        mean = (means[0] + means[1] + means[2] + means[3]) * 0.25
        spread = st[0, g, 1] + st[1, g, 1] + st[2, g, 1] + st[3, g, 1]
        for m in means:
            spread = spread + (m - mean) * (m - mean) * (2.0 * BLK)
        inv = lax.rsqrt(spread / D + 1e-06)
        mean_s[g] = mean
        inv_s[g] = inv

        def scale(i, _):
            b = lax.div(i, 4)
            r = pl.ds(pl.multiple_of(lax.rem(i, 4) * W, 64), W)
            piece = xt[0, g, b, r, :].astype(F32).reshape(W // 8, 8, TG)
            unit = ((piece - mean[None]) * inv[None]).reshape(W, TG)
            gain = gcol[b, r, :]
            nt[g, b, r, :] = (unit * jnp.concatenate([gain, gain], axis=1)).astype(BF16)
            return 0

        lax.fori_loop(0, 8, scale, 0)
        put_part(0, gi, dot(wit[0], nt[g, 0]) + dot(wit[1], nt[g, 1]))

    def up_part(gi):
        g = group(gi)
        wait_sib(1, g)
        put_part(1, gi, dot(wo[0], xt[1, g, 0]) + dot(wo[1], xt[1, g, 1]))

    def summed(arr):
        total = po[arr]
        for k in range(1, 4):
            other = pr.at[arr, xo(k)]
            remote(other, other, p_s.at[arr, k], p_r.at[arr, xo(k)], sibling).wait_recv()
            total = total + pr[arr, xo(k)].astype(F32)
        return total

    def hg_copy(arr, k):
        return remote(hg.at[arr, q], hg.at[arr, q], hg_s.at[arr, k], hg_r.at[arr, q], dev(h, xo(k), z, yl, c))

    def finish_h():
        preact = summed(0)
        pre[...] = preact
        cumul, _ = gelu_parts(preact)
        hg[0, q] = (preact * cumul).astype(BF16)
        for k in range(1, 4):
            hg_copy(0, k).start()

    def sm_copy(stage):
        dst, to = ((smc, sibling), (smy, ypart))[stage]
        return remote(smo.at[stage], dst, sm_s.at[stage], sm_r.at[stage], to)

    def smz_copy(k):
        return remote(smo.at[2], smz.at[z], smz_s.at[k], smz_r.at[z], dev(h, q, zo(k), yl, c))

    def finish_g():
        grad_hidden = summed(1)
        preact = pre[...]
        cumul, dense = gelu_parts(preact)
        grad = (grad_hidden * (cumul + preact * dense)).astype(BF16)
        hg[1, q] = grad
        for k in range(1, 4):
            hg_copy(1, k).start()
        by_gain = split_rows(jnp.sum(srow[...], axis=0, keepdims=True))
        smo[0, 0] = jnp.broadcast_to(jnp.sum(dot(by_gain, grad), axis=0, keepdims=True), (8, TG))
        inner = jnp.sum(grad.astype(F32) * preact, axis=0, keepdims=True)
        smo[0, 1] = jnp.broadcast_to(inner, (8, TG))
        sm_copy(0).start()

    def small_1():
        sm_copy(0).wait_recv()
        smo[1] = smo[0] + smc[...]
        sm_copy(1).start()

    def small_2():
        sm_copy(1).wait_recv()
        smo[2] = smo[1] + smy[...]
        for k in range(1, 8):
            smz_copy(k).start()

    def b_copy(arr, g, b):
        return remote(bp.at[arr, g, b, 1 - c], br.at[arr, g, b], b_s.at[arr, g, b], b_r.at[arr, g, b], sibling)

    def back_part(arr, gi):
        g = group(gi)
        if gi:
            other = hg.at[arr, g]
            remote(other, other, hg_s.at[arr, gi], hg_r.at[arr, g], sibling).wait_recv()
        act = hg[arr, g]
        for b in range(2):
            for y2 in range(2):
                w = wot[b, y2 * 384 : (y2 + 1) * 384, :] if arr == 0 else wi[q + 4 * b, pl.ds(y2 * 384, 384), :]
                part = dot(w, act).astype(BF16)
                bp[arr, g, b, 0, y2] = part[:W]
                bp[arr, g, b, 1, y2] = part[W:]
            b_copy(arr, g, b).start()

    def rs_flags(rb, g, y2):
        from_up = (rb <= 2) | ((rb == 3) & (y2 == 0))
        from_down = (rb == 0) | (rb >= 6) | ((rb == 5) & (y2 == 1))
        to_down = ((rb >= 1) & (rb <= 3)) | ((rb == 4) & (y2 == 0))
        to_up = (rb >= 5) | ((rb == 4) & (y2 == 1))
        sink = rb == 0
        local = sink & (g == q) & (y2 == yl)
        return from_up, from_down, to_up, to_down, sink, local

    def rs_copies(b, arr, g, y2):
        piece = bp.at[arr, g, b, c, y2]
        c_down = remote(piece, rz.at[arr, g, b, y2, 0], rz_s.at[arr, g, b, y2], rz_r.at[arr, g, b, y2, 0], zminus)
        c_up = remote(piece, rz.at[arr, g, b, y2, 1], rz_s.at[arr, g, b, y2], rz_r.at[arr, g, b, y2, 1], zplus)
        c_fin = remote(piece, fin.at[arr, yl], fin_s.at[arr, g, y2], fin_r.at[arr, yl], dev(h, g, z, y2, c))
        return c_up, c_down, c_fin

    def rs_step(s, _):
        for b in range(2):
            rb, dist = place(b)
            n = s - LAG * (4 - dist)

            @pl.when((n >= 0) & (n < 16))
            def _():
                arr, g, y2 = ag_item(n)
                from_up, from_down, to_up, to_down, sink, local = rs_flags(rb, g, y2)
                c_up, c_down, c_fin = rs_copies(b, arr, g, y2)

                @pl.when(y2 == 0)
                def _():
                    b_copy(arr, g, b).wait_recv()

                acc[...] = bp[arr, g, b, c, y2].astype(F32) + br[arr, g, b, y2].astype(F32)

                @pl.when(from_up)
                def _():
                    c_down.wait_recv()
                    acc[...] += rz[arr, g, b, y2, 0].astype(F32)

                @pl.when(from_down)
                def _():
                    c_up.wait_recv()
                    acc[...] += rz[arr, g, b, y2, 1].astype(F32)

                bp[arr, g, b, c, y2] = acc[...].astype(BF16)
                pl.when(to_up)(c_up.start)
                pl.when(to_down)(c_down.start)
                pl.when(sink & jnp.logical_not(local))(c_fin.start)

                @pl.when(local)
                def _():
                    fin[arr, yl] = acc[...].astype(BF16)

        return 0

    def rs_steps(lo, hi):
        lax.fori_loop(lo, hi, rs_step, 0)

    def gr_copy(i):
        return remote((gs, gso)[i].at[0], (gr, gro)[i].at[0], gr_s.at[i], gr_r.at[i], hpart)

    def grad_out_part():
        for t in range(2):
            other = sum(dot_t(hg[0, g], xt[1, g, 1 - h, pl.ds(t * 384, 384), :]) for g in range(4))
            gso[0, :, t * 384 : (t + 1) * 384] = other.astype(BF16)
        gr_copy(1).start()
        for t in range(2):
            go_ref[:, t * 384 : (t + 1) * 384] = sum(
                dot_t(hg[0, g], xt[1, g, h, pl.ds(t * 384, 384), :]) for g in range(4)
            )

    def grad_in_part():
        for t in range(2):
            other = sum(dot_t(nt[g, 1 - h, pl.ds(t * 384, 384), :], hg[1, g]) for g in range(4))
            gs[0, t * 384 : (t + 1) * 384, :] = other.astype(BF16)
        gr_copy(0).start()
        for t in range(2):
            gi_ref[t * 384 : (t + 1) * 384, :] = sum(
                dot_t(nt[g, h, pl.ds(t * 384, 384), :], hg[1, g]) for g in range(4)
            )

    base = 4 * LAG
    ag_steps(9, base + 2)
    for i in range(4):
        stats(i)
        ag_steps(base + 2 + 2 * i, base + 4 + 2 * i)
    norm_part(1)
    up_part(0)
    norm_part(2)
    ag_steps(base + 10, base + 12)
    norm_part(3)
    up_part(1)
    norm_part(0)
    ag_steps(base + 12, base + 14)
    up_part(2)
    ag_steps(base + 14, base + 16)
    up_part(3)
    finish_h()
    back_part(0, 0)
    back_part(0, 1)
    rs_steps(0, 2)
    finish_g()
    back_part(0, 2)
    rs_steps(2, 4)
    small_1()
    back_part(0, 3)
    rs_steps(4, 6)
    grad_out_part()
    small_2()
    back_part(1, 0)
    rs_steps(6, 8)
    back_part(1, 1)
    rs_steps(8, 10)
    back_part(1, 2)
    rs_steps(10, 12)
    back_part(1, 3)
    rs_steps(12, 14)
    grad_in_part()
    rs_steps(14, base + 16)

    def fin_wait(arr):
        for y2 in range(2):

            @pl.when(jnp.logical_not((xs == q) & (yl == y2)))
            def _():
                piece = fin.at[arr, y2]
                remote(piece, piece, fin_s.at[arr, 0, y2], fin_r.at[arr, y2], sibling).wait_recv()

    fin_wait(0)
    out_ref[...] = (x_ref[...].astype(F32) + (fin[0, 0].astype(F32) + fin[0, 1].astype(F32))).astype(BF16)

    sums = smo[2]
    for k in range(1, 8):
        remote(smz.at[zo(k)], smz.at[zo(k)], smz_s.at[k], smz_r.at[zo(k)], sibling).wait_recv()
        sums = sums + smz[zo(k)]
    mean, inv = mean_s[q][None], inv_s[q][None]
    unit = (x_ref[...].astype(F32).reshape(W // 8, 8, TG) - mean) * inv
    gain = gzcol[rows(yl, c), :]
    gain = jnp.concatenate([gain, gain], axis=1)
    fin_wait(1)
    scaled = ((fin[1, 0].astype(F32) + fin[1, 1].astype(F32)) * gain).reshape(W // 8, 8, TG)
    grad_ln = inv * (scaled - (sums[0] / D)[None] - unit * (sums[1] / D)[None])
    gt_ref[...] = (u_ref[...].astype(F32) + grad_ln.reshape(W, TG)).astype(BF16)

    gr_copy(0).wait_recv()
    gi_ref[...] += gr[0].astype(F32)
    gr_copy(1).wait_recv()
    go_ref[...] += gro[0].astype(F32)

    for arr in range(2):
        pl.when(xs != q)(origin(arr, 0).wait_send)
        origin(arr, 1).wait_send()
        for k in range(1, 4):
            hg_copy(arr, k).wait_send()
            p_copy(arr, k).wait_send()
    for i in range(2):
        gr_copy(i).wait_send()
        sm_copy(i).wait_send()
    for k in range(1, 8):
        smz_copy(k).wait_send()

    def drain(n, _):
        for b in range(2):
            rb, _ = place(b)
            up, down, _, c_up, c_down, c_sib = ag_copies(b, rb, n)
            pl.when(up)(c_up.wait_send)
            pl.when(down)(c_down.wait_send)
            c_sib.wait_send()
            arr, g, y2 = ag_item(n)
            _, _, to_up, to_down, sink, local = rs_flags(rb, g, y2)
            c_up, c_down, c_fin = rs_copies(b, arr, g, y2)
            pl.when(to_up)(c_up.wait_send)
            pl.when(to_down)(c_down.wait_send)
            pl.when(sink & jnp.logical_not(local))(c_fin.wait_send)
            pl.when(y2 == 0)(b_copy(arr, g, b).wait_send)
        return 0

    lax.fori_loop(0, 16, drain, 0)

    def drain_st(g, _):
        for k in range(1, 4):
            st_copy(g, k).wait_send()
        return 0

    lax.fori_loop(0, 4, drain_st, 0)


def body(tokens, upstream, norm_gain, w_in, w_out):
    sem = pltpu.SemaphoreType.DMA
    vmem = pl.BlockSpec(memory_space=pltpu.VMEM)
    hbm = pl.BlockSpec(memory_space=pl.ANY)
    scratch = [
        pltpu.VMEM((2, 4, 2, BLK, TG), BF16),
        pltpu.VMEM((4, 2, BLK, TG), BF16),
        pltpu.VMEM((8, BLK, FB), BF16),
        pltpu.VMEM((2, FB, BLK), BF16),
        pltpu.VMEM((2, FB, BLK), BF16),
        pltpu.VMEM((2, BLK, FB), BF16),
        pltpu.VMEM((2, BLK, 128), F32),
        pltpu.VMEM((BLK, 128), F32),
        pltpu.VMEM((16, FB), F32),
        pltpu.VMEM((4, 4, 2, 8, TG), F32),
        pltpu.VMEM((4, 8, TG), F32),
        pltpu.VMEM((4, 8, TG), F32),
        pltpu.VMEM((2, 4, FB, TG), BF16),
        pltpu.VMEM((2, 4, FB, TG), BF16),
        pltpu.VMEM((2, FB, TG), F32),
        pltpu.VMEM((FB, TG), F32),
        pltpu.VMEM((2, 4, FB, TG), BF16),
        pltpu.VMEM((2, 4, 2, 2, 2, W, TG), BF16),
        pltpu.VMEM((2, 4, 2, 2, W, TG), BF16),
        pltpu.VMEM((2, 4, 2, 2, 2, W, TG), BF16),
        pltpu.VMEM((W, TG), F32),
        pltpu.VMEM((2, 2, W, TG), BF16),
        pltpu.VMEM((3, 2, 8, TG), F32),
        pltpu.VMEM((2, 8, TG), F32),
        pltpu.VMEM((2, 8, TG), F32),
        pltpu.VMEM((8, 2, 8, TG), F32),
        pltpu.VMEM((1, BLK, FB), BF16),
        pltpu.VMEM((1, BLK, FB), BF16),
        pltpu.VMEM((1, FB, BLK), BF16),
        pltpu.VMEM((1, FB, BLK), BF16),
        sem((10,)),
        sem((2, 2)),
        sem((2, 4, 2, 2)),
        sem((2, 4, 2, 2, 2)),
        sem((2, 4, 2, 2)),
        sem((2, 4, 2, 2)),
        sem((4, 4)),
        sem((4, 4)),
        sem((2, 4)),
        sem((2, 4)),
        sem((2, 4)),
        sem((2, 4)),
        sem((2, 4, 2)),
        sem((2, 4, 2)),
        sem((2, 4, 2, 2)),
        sem((2, 4, 2, 2, 2)),
        sem((2, 4, 2)),
        sem((2, 2)),
        sem((2,)),
        sem((2,)),
        sem((8,)),
        sem((8,)),
        sem((2,)),
        sem((2,)),
    ]
    out_t, grad_t, grad_in, grad_out = pl.pallas_call(
        kernel,
        out_shape=(
            jax.ShapeDtypeStruct((W, TG), BF16),
            jax.ShapeDtypeStruct((W, TG), BF16),
            jax.ShapeDtypeStruct((BLK, FB), F32),
            jax.ShapeDtypeStruct((FB, BLK), F32),
        ),
        in_specs=[vmem, vmem, vmem, hbm, hbm],
        out_specs=(vmem, vmem, vmem, vmem),
        scratch_shapes=scratch,
        compiler_params=pltpu.CompilerParams(
            collective_id=1, has_side_effects=True, vmem_limit_bytes=58 << 20
        ),
        name="block",
    )(tokens.T, upstream.T, norm_gain.reshape(8, BLK), w_in, w_out)
    return out_t.T, grad_t.T, grad_in, grad_out


def solution(mesh):
    return jax.shard_map(
        body,
        mesh=mesh,
        in_specs=(P("dp", "mp"), P("dp", "mp"), P(), P(None, "mp"), P("mp", None)),
        out_specs=(P("dp", "mp"), P("dp", "mp"), P("dp", "mp"), P("mp", "dp")),
        check_vma=False,
    )
```

time: 709 us -> 162 us (0.23)
  the two profiles are of different devices: /device:TPU:10 before, /device:TPU:88 now
where the time goes in v1:
time: 162 us
  Pallas kernels  154 us (95%)
  local copies, waits for them, and re-layouts  7.9 us (5%)
    pallas_call x1, Pallas kernels, body(): pl.pallas_call(kernel, out_shape=(jax.ShapeDtypeStruct((W, TG), BF16), ja...  154 us
    unnamed x6, local copies, waits for them, and re-layouts  6.55 us

profile of v1, /device:TPU:88, one launch (start us, length us, event | category | flops | bytes accessed | tf_op | source)
XLA Modules:
  0.0 162.2 jit_solution(18129458328834149267)
XLA Ops:
  0.6 1.4 reshape.11.gain_ref
  2.0 153.6 %block.1 = (bf16[192,256]{1,0:T(8,128)(2,1)}, bf16[192,256]{1,0:T(8,128)(2,1)}, f32[768,384]{1,0:T(8,128)}, f32[384,768]{1,0:T(8,128)}) custom-call(bf16[192,256]{1,0:T(8,128)(2,1)} %bitcast.4, bf16[192,256]{1,0:T(8,128)(2,1)} %bitcast.5, f32[8,768]{1,0:T(8,128)} %reshape.11.gain_ref, bf16[6144,384]{1,0:T(8,128)(2,1)} %w_in_ref.1, bf16[384,6144]{1,0:T(8,128)(2,1)} %w_out_ref.1), custom_call_target="tpu_custom_call" | custom-call | tf_op jit(solution)/shard_map/block/pallas_call | solution.py:612
  155.6 1.5 copy.13
  157.1 1.5 copy.14
  158.7 0.0 copy-start
  158.7 2.5 %copy.15 = f32[768,384]{1,0:T(8,128)} copy(f32[768,384]{1,0:T(8,128)} %get-tuple-element.18) | data formatting | bytes 2359296
  161.1 0.0 copy-done
  161.1 1.0 copy.16
Async XLA Ops:
  158.7 2.5 %copy-start = (f32[384,768]{1,0:T(8,128)S(1)}, f32[384,768]{1,0:T(8,128)}, u32[]{:S(2)}) copy-start(f32[384,768]{1,0:T(8,128)} %get-tuple-element.19) | copy-start | bytes 3538948

commit v2 on v1

v2 whole, which is shorter than its diff:
```python
import functools

import jax
import jax.numpy as jnp
from jax import lax
from jax.experimental import pallas as pl
from jax.experimental.pallas import tpu as pltpu
from jax.sharding import PartitionSpec as P

MESH = pl.DeviceIdType.MESH
F32, BF16 = jnp.float32, jnp.bfloat16
D = 6144
BLK = 768
W = 192
TG = 256
FB = 384
ORDER = ((0, 2, 3, 1), (3, 1, 0, 2))
AG_ALONE = 1
RS_ALONE = 0
AG_ITEMS = 6 if AG_ALONE else 8
RS_ITEMS = 6 if RS_ALONE else 8
LAG = 2
YLAG = 2
RYLAG = 2
FILL = 4 * LAG
EXTRA = YLAG - 2 if AG_ALONE else 0
AG_END = 2 * AG_ITEMS + FILL + EXTRA
RS_START = 22
RS_END = RS_START + 2 * RS_ITEMS + FILL
LATE = 5
BACK = (0, 2, 4, 6)
GRAD_OUT = RS_START + 6
GRAD_IN = RS_START + 14


def gelu_parts(v):
    cumul = 0.5 * (1.0 + lax.erf(v * 0.7071067811865476))
    dense = jnp.exp(-0.5 * v * v) * 0.3989422804014327
    return cumul, dense


def split_rows(row):
    n = row.shape[1]
    hi = row.astype(BF16).astype(F32)
    mid = (row - hi).astype(BF16).astype(F32)
    low = row - hi - mid
    index = lax.broadcasted_iota(jnp.int32, (16, n), 0)
    spread = [jnp.broadcast_to(v, (16, n)) for v in (hi, mid, low)]
    zero = jnp.zeros((16, n), F32)
    out = jnp.where(
        index == 0, spread[0], jnp.where(index == 1, spread[1], jnp.where(index == 2, spread[2], zero))
    )
    return out.astype(BF16)


def column(row):
    return jnp.broadcast_to(row, (128, row.shape[1])).T


def dot(a, b):
    return jnp.dot(a, b, preferred_element_type=F32)


def dot_t(a, b):
    return lax.dot_general(a, b, (((1,), (1,)), ((), ())), preferred_element_type=F32)


def kernel(
    x_ref, u_ref, gain_ref, w_in_ref, w_out_ref,
    out_ref, gt_ref, gi_ref, go_ref,
    xt, nt, wi, wit, wo, wot, gcol, gzcol, srow,
    gain8, st, stm, stz, stx, ps, pr, po, pre, hg,
    bp, br, rz, ry, acc, fin, smo, smc, smy, smz, gs, gr, gso, gro, gi_own, go_own, out_own, gt_own,
    loc_sem, org_s, ag_r, ag_z, ag_y, sib_s, sib_r, st_s, st_r, stz_s, stz_r, stx_s, stx_r, p_s, p_r, hg_s, hg_r,
    b_s, b_r, rz_s, rz_r, ry_s, ry_r, fin_s, fin_r, sm_s, sm_r, smz_s, smz_r, gr_s, gr_r, out_sem,
):
    dp, mp = lax.axis_index("dp"), lax.axis_index("mp")
    h, q = lax.div(dp, 4), lax.rem(dp, 4)
    z, yl, c = lax.div(mp, 4), lax.rem(lax.div(mp, 2), 2), lax.rem(mp, 2)

    def dev(h_, x_, z_, y_, c_):
        return (h_ * 4 + x_, z_ * 4 + y_ * 2 + c_)

    def xo(k):
        return lax.rem(q + k, 4)

    def zo(k):
        return lax.rem(z + k, 8)

    sibling = dev(h, q, z, yl, 1 - c)
    ypart = dev(h, q, z, 1 - yl, c)
    hpart = dev(1 - h, q, z, yl, c)
    zplus, zminus = dev(h, q, zo(1), yl, c), dev(h, q, zo(7), yl, c)

    def remote(src, dst, ss, rs, to):
        return pltpu.make_async_remote_copy(
            src_ref=src, dst_ref=dst, send_sem=ss, recv_sem=rs, device_id=to, device_id_type=MESH
        )

    def wi_copy(k):
        return pltpu.make_async_copy(w_in_ref.at[pl.ds(k * BLK, BLK)], wi.at[k], loc_sem.at[k])

    def wo_copy(b):
        start = pl.multiple_of((q + 4 * b) * BLK, BLK)
        return pltpu.make_async_copy(w_out_ref.at[:, pl.ds(start, BLK)], wo.at[b], loc_sem.at[8 + b])

    for k in range(8):
        wi_copy(k).start()
    for b in range(2):
        wo_copy(b).start()

    partners = [sibling, ypart, hpart]
    partners += [dev(h, q, zo(k), yl, c) for k in range(1, 8)]
    partners += [dev(h, xo(k), z, y_, c) for k in range(1, 4) for y_ in (yl, 1 - yl)]
    barrier = pltpu.get_barrier_semaphore()
    for p in partners:
        pl.semaphore_signal(barrier, inc=1, device_id=p, device_id_type=MESH)
    pl.semaphore_wait(barrier, len(partners))

    def rows(y2, cc):
        return pl.ds(pl.multiple_of(y2 * 384 + cc * W, 64), W)

    xs = lax.rem(z, 4)
    zb = lax.div(z, 4)
    mine = (x_ref, u_ref)

    def own_only(k):
        return (k == 0) | (k == 3) if AG_ALONE else k < 0

    from_xs = lax.rem(q - xs + 4, 4)

    def origin(arr, other):
        to = dev(h, xs, z, 1 - yl if other else yl, c)
        return remote(
            mine[arr], xt.at[arr, q, zb, rows(yl, c)], org_s.at[arr, other], ag_r.at[arr, q, zb, yl], to
        )

    for arr in range(2):
        pl.when(xs != q)(origin(arr, 0).start)
        pl.when(jnp.logical_not(own_only(from_xs)))(origin(arr, 1).start)

    @pl.when(xs == q)
    def _():
        for arr in range(2):
            xt[arr, q, zb, rows(yl, c), :] = mine[arr][...]

    def st_copy(stage):
        return remote(st.at[stage], stm.at[stage], st_s.at[stage], st_r.at[stage], (sibling, ypart)[stage])

    def stz_copy(k):
        return remote(st.at[2], stz.at[z], stz_s.at[k], stz_r.at[z], dev(h, q, zo(k), yl, c))

    def stx_copy(k):
        return remote(stx.at[q], stx.at[q], stx_s.at[k], stx_r.at[q], dev(h, xo(k), z, yl, c))

    def own_stats():
        piece = x_ref[...].astype(F32).reshape(W // 8, 8, TG)
        total = jnp.sum(jnp.sum(piece, axis=0), axis=0, keepdims=True)
        mean = jnp.broadcast_to(total * (1.0 / W), (8, TG))
        d = piece - mean[None]
        st[0, 0] = mean
        spread = jnp.sum(jnp.sum(d * d, axis=0), axis=0, keepdims=True)
        st[0, 1] = jnp.broadcast_to(spread, (8, TG))
        st_copy(0).start()

    def merge(parts, count):
        mean = sum(p[0] for p in parts) * (1.0 / len(parts))
        spread = sum(p[1] for p in parts)
        for p in parts:
            spread = spread + (p[0] - mean) * (p[0] - mean) * float(count)
        return mean, spread

    def merge_pair(stage):
        st_copy(stage).wait_recv()
        parts = [(st[stage, 0], st[stage, 1]), (stm[stage, 0], stm[stage, 1])]
        st[stage + 1, 0], st[stage + 1, 1] = merge(parts, W * (stage + 1))
        if stage == 0:
            st_copy(1).start()
        else:
            for k in range(1, 8):
                stz_copy(k).start()

    def merge_z():
        parts = [(st[2, 0], st[2, 1])]
        for k in range(1, 8):
            other = stz.at[zo(k)]
            remote(other, other, stz_s.at[k], stz_r.at[zo(k)], sibling).wait_recv()
            parts.append((stz[zo(k), 0], stz[zo(k), 1]))
        mean, spread = merge(parts, 4 * W)
        stx[q, 0] = mean
        stx[q, 1] = lax.rsqrt(spread / D + 1e-06)
        for k in range(1, 4):
            stx_copy(k).start()

    own_stats()

    odd = lax.rem(q, 2)

    def offset(turn):
        off = [jnp.where(odd == 1, ORDER[1][i], ORDER[0][i]) for i in range(4)]
        if isinstance(turn, int):
            return off[turn]
        return jnp.where(turn < 2, jnp.where(turn == 0, off[0], off[1]), jnp.where(turn == 2, off[2], off[3]))

    def item(n, single):
        if AG_ALONE if single == 0 else RS_ALONE:
            arr, m = lax.div(n, 6), lax.rem(n, 6)
            pair, w = lax.div(m, 3), lax.rem(m, 3)
            alone = w == (0 if single == 0 else 2)
            turn = 2 * pair + jnp.where(alone, single, 1 - single)
            y2 = jnp.where(alone, yl, w - (1 if single == 0 else 0))
        else:
            arr, m = lax.div(n, 8), lax.rem(n, 8)
            turn, y2, alone = lax.div(m, 2), lax.rem(m, 2), m < 0
        return arr, xo(offset(turn)), y2, alone

    def place(b):
        rb = lax.rem(z - q + 8 - 4 * b, 8)
        return rb, jnp.minimum(rb, 8 - rb)

    def sib_copy(arr, g, b, y2, cc):
        piece = xt.at[arr, g, b, rows(y2, cc)]
        return remote(piece, piece, sib_s.at[arr, g, b, y2], sib_r.at[arr, g, b, y2], sibling)

    def ag_copies(b, rb, n):
        arr, g, y2, alone = item(n, 0)
        piece = xt.at[arr, g, b, rows(y2, c)]
        recv = ag_r.at[arr, g, b, y2]
        up = (rb <= 2) | ((rb == 3) & (y2 == 0))
        down = (rb == 0) | (rb >= 6) | ((rb == 5) & (y2 == 1))
        local = (rb == 0) & (g == q) & (y2 == yl)
        c_up = remote(piece, piece, ag_z.at[arr, g, b, y2, 0], recv, zplus)
        c_down = remote(piece, piece, ag_z.at[arr, g, b, y2, 1], recv, zminus)
        c_y = remote(piece, piece, ag_y.at[arr, g, b], recv, ypart)
        return up, down, local, alone, c_up, c_down, c_y, sib_copy(arr, g, b, y2, c)

    def ag_step(s):
        for b in range(2):
            rb, dist = place(b)
            n = s - LAG * dist

            @pl.when((n >= 0) & (n < 2 * AG_ITEMS))
            def _():
                up, down, local, alone, c_up, c_down, c_y, c_sib = ag_copies(b, rb, n)

                @pl.when(jnp.logical_not(local))
                def _():
                    c_up.wait_recv()

                pl.when(up)(c_up.start)
                pl.when(down)(c_down.start)
                pl.when(alone)(c_y.start)
                c_sib.start()

        for b in range(2):
            _, dist = place(b)
            late = s - LAG * dist - YLAG

            @pl.when((late >= 0) & (late < 2 * AG_ITEMS))
            def _():
                arr, g, _, alone = item(late, 0)

                @pl.when(alone)
                def _():
                    c_sib = sib_copy(arr, g, b, 1 - yl, c)
                    piece = xt.at[arr, g, b, rows(1 - yl, c)]
                    remote(piece, piece, ag_y.at[arr, g, b], ag_r.at[arr, g, b, 1 - yl], ypart).wait_recv()
                    c_sib.start()

    def prep_wi(b):
        for k in range(4 * b, 4 * b + 4):
            wi_copy(k).wait()

    def prep_s(lo, hi):
        for k in range(lo, hi):
            term = dot(split_rows(gain8[k : k + 1, :]), wi[k])
            if k == 0:
                srow[...] = term
            else:
                srow[...] += term

    def prep_wit(b):
        for t in range(2):
            part = wi[q + 4 * b, pl.ds(t * 384, 384), :]
            wit[b, :, t * 384 : (t + 1) * 384] = part.T

    def prep_wot(b):
        wo_copy(b).wait()
        for t in range(2):
            wot[b, t * 384 : (t + 1) * 384, :] = wo[b, :, t * 384 : (t + 1) * 384].T

    def prep_gain():
        for k in range(8):
            gain8[k : k + 1, :] = gain_ref[k * BLK : (k + 1) * BLK].reshape(1, BLK)
        for b in range(2):
            gcol[b] = column(gain8[pl.ds(q + 4 * b, 1), :])
        gzcol[...] = column(gain8[pl.ds(z, 1), :])

    def wait_sib(arr, g):
        for b in range(2):
            for y2 in range(2):
                sib_copy(arr, g, b, y2, 1 - c).wait_recv()

    def p_copy(arr, k):
        return remote(ps.at[arr, xo(k)], pr.at[arr, q], p_s.at[arr, k], p_r.at[arr, q], dev(h, xo(k), z, yl, c))

    def put_part(arr, k, part):
        @pl.when(k == 0)
        def _():
            po[arr] = part

        @pl.when(k > 0)
        def _():
            ps[arr, xo(k)] = part.astype(BF16)
            p_copy(arr, k).start()

    def norm_part(turn):
        k = offset(turn)
        g = xo(k)
        wait_sib(0, g)

        @pl.when(k > 0)
        def _():
            other = stx.at[g]
            remote(other, other, stx_s.at[k], stx_r.at[g], sibling).wait_recv()

        mean, inv = stx[g, 0], stx[g, 1]

        def scale(i, _):
            b = lax.div(i, 4)
            r = pl.ds(pl.multiple_of(lax.rem(i, 4) * W, 64), W)
            piece = xt[0, g, b, r, :].astype(F32).reshape(W // 8, 8, TG)
            unit = ((piece - mean[None]) * inv[None]).reshape(W, TG)
            gain = gcol[b, r, :]
            nt[g, b, r, :] = (unit * jnp.concatenate([gain, gain], axis=1)).astype(BF16)
            return 0

        lax.fori_loop(0, 8, scale, 0)
        put_part(0, k, dot(wit[0], nt[g, 0]) + dot(wit[1], nt[g, 1]))

    def up_part(turn):
        k = offset(turn)
        g = xo(k)
        wait_sib(1, g)
        put_part(1, k, dot(wo[0], xt[1, g, 0]) + dot(wo[1], xt[1, g, 1]))

    def summed(arr):
        total = po[arr]
        for k in range(1, 4):
            other = pr.at[arr, xo(k)]
            remote(other, other, p_s.at[arr, k], p_r.at[arr, xo(k)], sibling).wait_recv()
            total = total + pr[arr, xo(k)].astype(F32)
        return total

    def hg_copy(arr, k):
        return remote(hg.at[arr, q], hg.at[arr, q], hg_s.at[arr, k], hg_r.at[arr, q], dev(h, xo(k), z, yl, c))

    def last_h():
        preact = summed(0)
        pre[...] = preact
        cumul, _ = gelu_parts(preact)
        hg[0, q] = (preact * cumul).astype(BF16)
        for k in (1, 3, 2):
            hg_copy(0, k).start()

    def sm_copy(stage):
        dst, to = ((smc, sibling), (smy, ypart))[stage]
        return remote(smo.at[stage], dst, sm_s.at[stage], sm_r.at[stage], to)

    def smz_copy(k):
        return remote(smo.at[2], smz.at[z], smz_s.at[k], smz_r.at[z], dev(h, q, zo(k), yl, c))

    def last_g():
        grad_hidden = summed(1)
        preact = pre[...]
        cumul, dense = gelu_parts(preact)
        grad = (grad_hidden * (cumul + preact * dense)).astype(BF16)
        hg[1, q] = grad
        for k in (1, 3, 2):
            hg_copy(1, k).start()
        by_gain = split_rows(jnp.sum(srow[...], axis=0, keepdims=True))
        smo[0, 0] = jnp.broadcast_to(jnp.sum(dot(by_gain, grad), axis=0, keepdims=True), (8, TG))
        inner = jnp.sum(grad.astype(F32) * preact, axis=0, keepdims=True)
        smo[0, 1] = jnp.broadcast_to(inner, (8, TG))
        sm_copy(0).start()

    def finish_h(slot):
        pl.when(odd == slot)(last_h)

    def finish_g(slot):
        pl.when(odd == slot)(last_g)

    def small_1():
        sm_copy(0).wait_recv()
        smo[1] = smo[0] + smc[...]
        sm_copy(1).start()

    def small_2():
        sm_copy(1).wait_recv()
        smo[2] = smo[1] + smy[...]
        for k in range(1, 8):
            smz_copy(k).start()

    def b_copy(arr, g, b):
        return remote(bp.at[arr, g, b, 1 - c], br.at[arr, g, b], b_s.at[arr, g, b], b_r.at[arr, g, b], sibling)

    def back_part(arr, turn):
        k = offset(turn)
        g = xo(k)

        @pl.when(k > 0)
        def _():
            other = hg.at[arr, g]
            remote(other, other, hg_s.at[arr, k], hg_r.at[arr, g], sibling).wait_recv()
        act = hg[arr, g]
        for b in range(2):
            for y2 in range(2):
                w = wot[b, y2 * 384 : (y2 + 1) * 384, :] if arr == 0 else wi[q + 4 * b, pl.ds(y2 * 384, 384), :]
                part = dot(w, act).astype(BF16)
                bp[arr, g, b, 0, y2] = part[:W]
                bp[arr, g, b, 1, y2] = part[W:]
            b_copy(arr, g, b).start()

    def rs_flags(rb, g, y2):
        from_up = (rb <= 2) | ((rb == 3) & (y2 == 0))
        from_down = (rb == 0) | (rb >= 6) | ((rb == 5) & (y2 == 1))
        to_down = ((rb >= 1) & (rb <= 3)) | ((rb == 4) & (y2 == 0))
        to_up = (rb >= 5) | ((rb == 4) & (y2 == 1))
        sink = rb == 0
        local = sink & (g == q) & (y2 == yl)
        return from_up, from_down, to_up, to_down, sink, local

    def rs_copies(b, arr, g, y2):
        piece = bp.at[arr, g, b, c, y2]
        sent, got = rz_s.at[arr, g, b, y2], rz_r.at[arr, g, b, y2]
        c_down = remote(piece, rz.at[arr, g, b, y2, 0], sent, got.at[0], zminus)
        c_up = remote(piece, rz.at[arr, g, b, y2, 1], sent, got.at[1], zplus)
        c_fin = remote(piece, fin.at[arr, yl], fin_s.at[arr, g, y2], fin_r.at[arr, yl], dev(h, g, z, y2, c))
        return c_up, c_down, c_fin

    def ry_copy(arr, g, b):
        return remote(bp.at[arr, g, b, c, 1 - yl], ry.at[arr, g, b], ry_s.at[arr, g, b], ry_r.at[arr, g, b], ypart)

    def rs_step(s):
        for b in range(2):
            rb, dist = place(b)
            n = s - LAG * (4 - dist)
            early = n + RYLAG

            @pl.when((early >= 0) & (early < 2 * RS_ITEMS))
            def _():
                arr, g, _, alone = item(early, 1)

                @pl.when(alone)
                def _():
                    b_copy(arr, g, b).wait_recv()
                    both = bp[arr, g, b, c, 1 - yl].astype(F32) + br[arr, g, b, 1 - yl].astype(F32)
                    bp[arr, g, b, c, 1 - yl] = both.astype(BF16)
                    ry_copy(arr, g, b).start()

            @pl.when((n >= 0) & (n < 2 * RS_ITEMS))
            def _():
                arr, g, y2, alone = item(n, 1)
                from_up, from_down, to_up, to_down, sink, local = rs_flags(rb, g, y2)
                c_up, c_down, c_fin = rs_copies(b, arr, g, y2)

                @pl.when((y2 == 0) & jnp.logical_not(alone))
                def _():
                    b_copy(arr, g, b).wait_recv()

                acc[...] = bp[arr, g, b, c, y2].astype(F32) + br[arr, g, b, y2].astype(F32)

                @pl.when(alone)
                def _():
                    ry_copy(arr, g, b).wait_recv()
                    acc[...] += ry[arr, g, b].astype(F32)

                @pl.when(from_up)
                def _():
                    c_down.wait_recv()
                    acc[...] += rz[arr, g, b, y2, 0].astype(F32)

                @pl.when(from_down)
                def _():
                    c_up.wait_recv()
                    acc[...] += rz[arr, g, b, y2, 1].astype(F32)

                bp[arr, g, b, c, y2] = acc[...].astype(BF16)
                pl.when(to_up)(c_up.start)
                pl.when(to_down)(c_down.start)
                pl.when(sink & jnp.logical_not(local))(c_fin.start)

                @pl.when(local)
                def _():
                    fin[arr, yl] = acc[...].astype(BF16)

    def gr_copy(i):
        return remote((gs, gso)[i].at[0], (gr, gro)[i].at[0], gr_s.at[i], gr_r.at[i], hpart)

    def grad_out_sent():
        for t in range(2):
            other = sum(dot_t(hg[0, g], xt[1, g, 1 - h, pl.ds(t * 384, 384), :]) for g in range(4))
            gso[0, :, t * 384 : (t + 1) * 384] = other.astype(BF16)
        gr_copy(1).start()

    def grad_out_own():
        for t in range(2):
            go_own[:, t * 384 : (t + 1) * 384] = sum(
                dot_t(hg[0, g], xt[1, g, h, pl.ds(t * 384, 384), :]) for g in range(4)
            )

    def grad_in_sent():
        for t in range(2):
            other = sum(dot_t(nt[g, 1 - h, pl.ds(t * 384, 384), :], hg[1, g]) for g in range(4))
            gs[0, t * 384 : (t + 1) * 384, :] = other.astype(BF16)
        gr_copy(0).start()

    def grad_in_own():
        for t in range(2):
            gi_own[t * 384 : (t + 1) * 384, :] = sum(
                dot_t(nt[g, h, pl.ds(t * 384, 384), :], hg[1, g]) for g in range(4)
            )

    turns = {}

    def at(step, run, *args):
        turns.setdefault(step, []).append(functools.partial(run, *args))

    at(1, merge_pair, 0)
    at(1, prep_wi, 0)
    at(2, prep_wi, 1)
    at(2, prep_gain)
    at(3, merge_pair, 1)
    for b in range(2):
        at(3 + b, prep_wit, b)
        at(6 + b, prep_wot, b)
        at(8 + b, prep_s, 4 * b, 4 * b + 4)
    at(5, merge_z)
    pair_a = AG_ITEMS // 2
    for i in range(4):
        at(FILL + pair_a * (i // 2 + 1) + EXTRA, norm_part, i)
        at(FILL + pair_a * (i // 2 + 3) + EXTRA, up_part, i)
        for arr in range(2):
            at(RS_START + RS_ITEMS * arr - 1 + BACK[i], back_part, arr, i)
    for slot in range(2):
        at(FILL + pair_a * (slot + 1) + LATE, finish_h, slot)
        at(FILL + pair_a * (slot + 3) + LATE, finish_g, slot)
    at(GRAD_OUT, grad_out_sent)
    at(RS_END - 4, grad_out_own)
    at(FILL + 2 * AG_ITEMS + LATE + 2, small_1)
    at(FILL + 2 * AG_ITEMS + LATE + 4, small_2)
    at(GRAD_IN, grad_in_sent)
    at(RS_END - 3, grad_in_own)

    def both(s, _):
        ag_step(s)
        rs_step(s - RS_START)
        return 0

    def first(s, _):
        ag_step(s)
        return 0

    def second(s, _):
        rs_step(s - RS_START)
        return 0

    marks = sorted(set(turns) | {0, RS_START, AG_END, RS_END})
    for lo, hi in zip(marks, marks[1:] + [RS_END]):
        for run in turns.get(lo, ()):
            run()
        if lo < hi:
            lax.fori_loop(lo, hi, first if lo < RS_START else both if lo < AG_END else second, 0)

    outs = ((gi_own, gi_ref), (go_own, go_ref), (out_own, out_ref), (gt_own, gt_ref))

    def put(i):
        return pltpu.make_async_copy(outs[i][0], outs[i][1], out_sem.at[i])

    gr_copy(1).wait_recv()
    go_own[...] += gro[0].astype(F32)
    put(1).start()
    gr_copy(0).wait_recv()
    gi_own[...] += gr[0].astype(F32)
    put(0).start()

    alone = (from_xs == 1) | (from_xs == 2) if RS_ALONE else from_xs < 0

    def fin_wait(arr):
        @pl.when(alone)
        def _():
            fin[arr, 1 - yl] = jnp.zeros((W, TG), BF16)

        for y2 in range(2):

            @pl.when(jnp.logical_not((xs == q) & (yl == y2)) & ((yl == y2) | jnp.logical_not(alone)))
            def _():
                piece = fin.at[arr, y2]
                remote(piece, piece, fin_s.at[arr, 0, y2], fin_r.at[arr, y2], sibling).wait_recv()

    fin_wait(0)
    out_own[...] = (x_ref[...].astype(F32) + (fin[0, 0].astype(F32) + fin[0, 1].astype(F32))).astype(BF16)

    sums = smo[2]
    for k in range(1, 8):
        remote(smz.at[zo(k)], smz.at[zo(k)], smz_s.at[k], smz_r.at[zo(k)], sibling).wait_recv()
        sums = sums + smz[zo(k)]
    mean, inv = stx[q, 0][None], stx[q, 1][None]
    unit = (x_ref[...].astype(F32).reshape(W // 8, 8, TG) - mean) * inv
    gain = gzcol[rows(yl, c), :]
    gain = jnp.concatenate([gain, gain], axis=1)
    fin_wait(1)
    scaled = ((fin[1, 0].astype(F32) + fin[1, 1].astype(F32)) * gain).reshape(W // 8, 8, TG)
    grad_ln = inv * (scaled - (sums[0] / D)[None] - unit * (sums[1] / D)[None])
    put(2).start()
    gt_own[...] = (u_ref[...].astype(F32) + grad_ln.reshape(W, TG)).astype(BF16)


    put(3).start()

    for arr in range(2):
        pl.when(xs != q)(origin(arr, 0).wait_send)
        pl.when(jnp.logical_not(own_only(from_xs)))(origin(arr, 1).wait_send)
        for k in range(1, 4):
            hg_copy(arr, k).wait_send()
            p_copy(arr, k).wait_send()
    for i in range(2):
        gr_copy(i).wait_send()
        sm_copy(i).wait_send()
    for k in range(1, 8):
        smz_copy(k).wait_send()

    def drain_ag(n, _):
        for b in range(2):
            rb, _ = place(b)
            up, down, _, alone, c_up, c_down, c_y, c_sib = ag_copies(b, rb, n)
            arr, g, _, _ = item(n, 0)
            pl.when(up)(c_up.wait_send)
            pl.when(down)(c_down.wait_send)
            c_sib.wait_send()

            @pl.when(alone)
            def _():
                c_y.wait_send()
                sib_copy(arr, g, b, 1 - yl, c).wait_send()

        return 0

    def drain_rs(n, _):
        for b in range(2):
            rb, _ = place(b)
            arr, g, y2, alone = item(n, 1)
            _, _, to_up, to_down, sink, local = rs_flags(rb, g, y2)
            c_up, c_down, c_fin = rs_copies(b, arr, g, y2)
            pl.when(to_up)(c_up.wait_send)
            pl.when(to_down)(c_down.wait_send)
            pl.when(sink & jnp.logical_not(local))(c_fin.wait_send)
            pl.when(alone)(ry_copy(arr, g, b).wait_send)
            pl.when((y2 == 0) | alone)(b_copy(arr, g, b).wait_send)
        return 0

    lax.fori_loop(0, 2 * AG_ITEMS, drain_ag, 0)
    lax.fori_loop(0, 2 * RS_ITEMS, drain_rs, 0)

    for k in range(1, 8):
        stz_copy(k).wait_send()
    for k in range(1, 4):
        stx_copy(k).wait_send()
    for i in range(2):
        st_copy(i).wait_send()
    for i in range(4):
        put(i).wait()


def finish(*refs):
    sources, results, held, sems = refs[:4], refs[4:8], refs[8:12], refs[12]
    jobs = []
    for i in range(4):
        size = sources[i].shape[0]
        step = size // (4 if i > 1 else 1)
        for t in range(0, size, step):
            part, k = pl.ds(t, step), len(jobs)
            jobs.append(
                (
                    pltpu.make_async_copy(sources[i].at[part], held[i].at[part], sems.at[0, k]),
                    pltpu.make_async_copy(held[i].at[part], results[i].at[part], sems.at[1, k]),
                )
            )
    for first, _ in jobs:
        first.start()
    for first, second in jobs:
        first.wait()
        second.start()
    for _, second in jobs:
        second.wait()


def body(tokens, upstream, norm_gain, w_in, w_out):
    sem = pltpu.SemaphoreType.DMA
    vmem = pl.BlockSpec(memory_space=pltpu.VMEM)
    hbm = pl.BlockSpec(memory_space=pl.ANY)
    scratch = [
        pltpu.VMEM((2, 4, 2, BLK, TG), BF16),
        pltpu.VMEM((4, 2, BLK, TG), BF16),
        pltpu.VMEM((8, BLK, FB), BF16),
        pltpu.VMEM((2, FB, BLK), BF16),
        pltpu.VMEM((2, FB, BLK), BF16),
        pltpu.VMEM((2, BLK, FB), BF16),
        pltpu.VMEM((2, BLK, 128), F32),
        pltpu.VMEM((BLK, 128), F32),
        pltpu.VMEM((16, FB), F32),
        pltpu.VMEM((8, BLK), F32),
        pltpu.VMEM((3, 2, 8, TG), F32),
        pltpu.VMEM((2, 2, 8, TG), F32),
        pltpu.VMEM((8, 2, 8, TG), F32),
        pltpu.VMEM((4, 2, 8, TG), F32),
        pltpu.VMEM((2, 4, FB, TG), BF16),
        pltpu.VMEM((2, 4, FB, TG), BF16),
        pltpu.VMEM((2, FB, TG), F32),
        pltpu.VMEM((FB, TG), F32),
        pltpu.VMEM((2, 4, FB, TG), BF16),
        pltpu.VMEM((2, 4, 2, 2, 2, W, TG), BF16),
        pltpu.VMEM((2, 4, 2, 2, W, TG), BF16),
        pltpu.VMEM((2, 4, 2, 2, 2, W, TG), BF16),
        pltpu.VMEM((2, 4, 2, W, TG), BF16),
        pltpu.VMEM((W, TG), F32),
        pltpu.VMEM((2, 2, W, TG), BF16),
        pltpu.VMEM((3, 2, 8, TG), F32),
        pltpu.VMEM((2, 8, TG), F32),
        pltpu.VMEM((2, 8, TG), F32),
        pltpu.VMEM((8, 2, 8, TG), F32),
        pltpu.VMEM((1, BLK, FB), BF16),
        pltpu.VMEM((1, BLK, FB), BF16),
        pltpu.VMEM((1, FB, BLK), BF16),
        pltpu.VMEM((1, FB, BLK), BF16),
        pltpu.VMEM((BLK, FB), F32),
        pltpu.VMEM((FB, BLK), F32),
        pltpu.VMEM((W, TG), BF16),
        pltpu.VMEM((W, TG), BF16),
        sem((10,)),
        sem((2, 2)),
        sem((2, 4, 2, 2)),
        sem((2, 4, 2, 2, 2)),
        sem((2, 4, 2)),
        sem((2, 4, 2, 2)),
        sem((2, 4, 2, 2)),
        sem((2,)),
        sem((2,)),
        sem((8,)),
        sem((8,)),
        sem((4,)),
        sem((4,)),
        sem((2, 4)),
        sem((2, 4)),
        sem((2, 4)),
        sem((2, 4)),
        sem((2, 4, 2)),
        sem((2, 4, 2)),
        sem((2, 4, 2, 2)),
        sem((2, 4, 2, 2, 2)),
        sem((2, 4, 2)),
        sem((2, 4, 2)),
        sem((2, 4, 2)),
        sem((2, 2)),
        sem((2,)),
        sem((2,)),
        sem((8,)),
        sem((8,)),
        sem((2,)),
        sem((2,)),
        sem((4,)),
    ]
    shapes = (
        jax.ShapeDtypeStruct((W, TG), BF16),
        jax.ShapeDtypeStruct((W, TG), BF16),
        jax.ShapeDtypeStruct((BLK, FB), F32),
        jax.ShapeDtypeStruct((FB, BLK), F32),
    )
    results = pl.pallas_call(
        kernel,
        out_shape=shapes,
        in_specs=[vmem, vmem, vmem, hbm, hbm],
        out_specs=(hbm,) * 4,
        scratch_shapes=scratch,
        compiler_params=pltpu.CompilerParams(
            collective_id=1, has_side_effects=True, vmem_limit_bytes=58 << 20
        ),
        name="block",
    )(tokens.T, upstream.T, norm_gain, w_in, w_out)
    out_t, grad_t, grad_in, grad_out = pl.pallas_call(
        finish,
        out_shape=shapes,
        in_specs=[hbm] * 4,
        out_specs=(hbm,) * 4,
        scratch_shapes=[pltpu.VMEM(a.shape, a.dtype) for a in shapes] + [sem((2, 10))],
        name="finish",
    )(*results)
    return out_t.T, grad_t.T, grad_in, grad_out


def solution(mesh):
    return jax.shard_map(
        body,
        mesh=mesh,
        in_specs=(P("dp", "mp"), P("dp", "mp"), P(), P(None, "mp"), P("mp", None)),
        out_specs=(P("dp", "mp"), P("dp", "mp"), P("dp", "mp"), P("mp", "dp")),
        check_vma=False,
    )
```

time: 162 us -> 137 us (0.85)
  the two profiles are of different devices: /device:TPU:88 before, /device:TPU:10 now
where the time goes in v2:
time: 137 us
  Pallas kernels  137 us (100%)
    pallas_call x1, Pallas kernels, body(): pl.pallas_call(kernel, out_shape=shapes, in_specs=[vmem, vmem, vmem, hbm,...  134 us

profile of v2, /device:TPU:10, one launch (start us, length us, event | category | flops | bytes accessed | tf_op | source)
XLA Modules:
  0.0 137.3 jit_solution(1840691484170297619)
XLA Ops:
  0.6 133.9 %block.1 = (bf16[192,256]{1,0:T(8,128)(2,1)}, bf16[192,256]{1,0:T(8,128)(2,1)}, f32[768,384]{1,0:T(8,128)}, f32[384,768]{1,0:T(8,128)}) custom-call(bf16[192,256]{1,0:T(8,128)(2,1)} %bitcast.4, bf16[192,256]{1,0:T(8,128)(2,1)} %bitcast.5, f32[6144]{0:T(1024)} %gain_ref.1, bf16[6144,384]{1,0:T(8,128)(2,1)} %w_in_ref.1, bf16[384,6144]{1,0:T(8,128)(2,1)} %w_out_ref.1), custom_call_target="tpu_custom_call" | custom-call | tf_op jit(solution)/shard_map/block/pallas_call | solution.py:779
  134.5 2.6 %finish.1 = (bf16[192,256]{1,0:T(8,128)(2,1)}, bf16[192,256]{1,0:T(8,128)(2,1)}, f32[768,384]{1,0:T(8,128)}, f32[384,768]{1,0:T(8,128)}) custom-call(bf16[192,256]{1,0:T(8,128)(2,1)} %get-tuple-element.12.refs_0_, bf16[192,256]{1,0:T(8,128)(2,1)} %get-tuple-element.13.refs_1_, f32[768,384]{1,0:T(8,128)} %get-tuple-element.14.refs_2_, ...), custom_call_target="tpu_custom_call" | custom-call | tf_op jit(solution)/shard_map/finish/pallas_call | solution.py:790

commit v3 on v2

--- a/solution.py
+++ b/solution.py
@@ -14,23 +14,47 @@
 W = 192
 TG = 256
 FB = 384
-ORDER = ((0, 2, 3, 1), (3, 1, 0, 2))
-AG_ALONE = 1
-RS_ALONE = 0
-AG_ITEMS = 6 if AG_ALONE else 8
-RS_ITEMS = 6 if RS_ALONE else 8
+ORDER = ((0, 2, 1, 3), (0, 2, 3, 1))
+HG_ORDER = (1, 3, 2)
+PLAN5 = ((0, 2), (1, 2), (2, 2), (3, 0), (3, 1))
+PLAN6 = ((0, 2), (1, 0), (1, 1), (2, 2), (3, 0), (3, 1))
+PLAN6R = ((0, 0), (0, 1), (1, 2), (2, 0), (2, 1), (3, 2))
+PLAN7R = ((0, 0), (0, 1), (1, 2), (2, 0), (2, 1), (3, 0), (3, 1))
+PLAN8 = tuple((t, y) for t in range(4) for y in range(2))
+AG_PLAN = PLAN5
+RS_PLAN = PLAN8
+AG_ITEMS = len(AG_PLAN)
+RS_ITEMS = len(RS_PLAN)
 LAG = 2
 YLAG = 2
 RYLAG = 2
 FILL = 4 * LAG
-EXTRA = YLAG - 2 if AG_ALONE else 0
-AG_END = 2 * AG_ITEMS + FILL + EXTRA
-RS_START = 22
+AG_END = 2 * AG_ITEMS + FILL
+RS_START = 21
 RS_END = RS_START + 2 * RS_ITEMS + FILL
 LATE = 5
-BACK = (0, 2, 4, 6)
+SLOTS = 0
+ORIGIN_U = 1
+BACK = ((0, 2, 4, 6), (0, 2, 4, 5))
 GRAD_OUT = RS_START + 6
-GRAD_IN = RS_START + 14
+GRAD_IN = RS_START + 12
+OWN = 4
+
+
+def alone_turns(plan):
+    return tuple(t for t, y in plan if y == 2)
+
+
+def done(arr, turn):
+    last = max(i + (YLAG if y == 2 else 0) for i, (t, y) in enumerate(AG_PLAN) if t == turn)
+    return FILL + arr * AG_ITEMS + last + 1
+
+
+def choose(table, i):
+    value = jnp.int32(table[-1])
+    for k in range(len(table) - 1):
+        value = jnp.where(i == k, jnp.int32(table[k]), value)
+    return value
 
 
 def gelu_parts(v):
@@ -124,8 +148,11 @@
     zb = lax.div(z, 4)
     mine = (x_ref, u_ref)
 
-    def own_only(k):
-        return (k == 0) | (k == 3) if AG_ALONE else k < 0
+    def own_only(plan, k, par):
+        out = k < 0
+        for t in alone_turns(plan):
+            out = out | (k == jnp.where(par == 1, ORDER[1][t], ORDER[0][t]))
+        return out
 
     from_xs = lax.rem(q - xs + 4, 4)
 
@@ -135,9 +162,13 @@
             mine[arr], xt.at[arr, q, zb, rows(yl, c)], org_s.at[arr, other], ag_r.at[arr, q, zb, yl], to
         )
 
-    for arr in range(2):
+    crosses = jnp.logical_not(own_only(AG_PLAN, from_xs, lax.rem(xs, 2)))
+
+    def origin_sends(arr):
         pl.when(xs != q)(origin(arr, 0).start)
-        pl.when(jnp.logical_not(own_only(from_xs)))(origin(arr, 1).start)
+        pl.when(crosses)(origin(arr, 1).start)
+
+    origin_sends(0)
 
     @pl.when(xs == q)
     def _():
@@ -202,17 +233,12 @@
             return off[turn]
         return jnp.where(turn < 2, jnp.where(turn == 0, off[0], off[1]), jnp.where(turn == 2, off[2], off[3]))
 
-    def item(n, single):
-        if AG_ALONE if single == 0 else RS_ALONE:
-            arr, m = lax.div(n, 6), lax.rem(n, 6)
-            pair, w = lax.div(m, 3), lax.rem(m, 3)
-            alone = w == (0 if single == 0 else 2)
-            turn = 2 * pair + jnp.where(alone, single, 1 - single)
-            y2 = jnp.where(alone, yl, w - (1 if single == 0 else 0))
-        else:
-            arr, m = lax.div(n, 8), lax.rem(n, 8)
-            turn, y2, alone = lax.div(m, 2), lax.rem(m, 2), m < 0
-        return arr, xo(offset(turn)), y2, alone
+    def item(n, plan):
+        arr, m = lax.div(n, len(plan)), lax.rem(n, len(plan))
+        half = choose([y for _, y in plan], m)
+        alone = half == 2
+        k = offset(choose([t for t, _ in plan], m))
+        return arr, xo(k), jnp.where(alone, yl, half), alone
 
     def place(b):
         rb = lax.rem(z - q + 8 - 4 * b, 8)
@@ -223,7 +249,7 @@
         return remote(piece, piece, sib_s.at[arr, g, b, y2], sib_r.at[arr, g, b, y2], sibling)
 
     def ag_copies(b, rb, n):
-        arr, g, y2, alone = item(n, 0)
+        arr, g, y2, alone = item(n, AG_PLAN)
         piece = xt.at[arr, g, b, rows(y2, c)]
         recv = ag_r.at[arr, g, b, y2]
         up = (rb <= 2) | ((rb == 3) & (y2 == 0))
@@ -247,10 +273,10 @@
                 def _():
                     c_up.wait_recv()
 
+                c_sib.start()
                 pl.when(up)(c_up.start)
                 pl.when(down)(c_down.start)
                 pl.when(alone)(c_y.start)
-                c_sib.start()
 
         for b in range(2):
             _, dist = place(b)
@@ -258,7 +284,7 @@
 
             @pl.when((late >= 0) & (late < 2 * AG_ITEMS))
             def _():
-                arr, g, _, alone = item(late, 0)
+                arr, g, _, alone = item(late, AG_PLAN)
 
                 @pl.when(alone)
                 def _():
@@ -360,7 +386,7 @@
         pre[...] = preact
         cumul, _ = gelu_parts(preact)
         hg[0, q] = (preact * cumul).astype(BF16)
-        for k in (1, 3, 2):
+        for k in HG_ORDER:
             hg_copy(0, k).start()
 
     def sm_copy(stage):
@@ -376,7 +402,7 @@
         cumul, dense = gelu_parts(preact)
         grad = (grad_hidden * (cumul + preact * dense)).astype(BF16)
         hg[1, q] = grad
-        for k in (1, 3, 2):
+        for k in HG_ORDER:
             hg_copy(1, k).start()
         by_gain = split_rows(jnp.sum(srow[...], axis=0, keepdims=True))
         smo[0, 0] = jnp.broadcast_to(jnp.sum(dot(by_gain, grad), axis=0, keepdims=True), (8, TG))
@@ -449,7 +475,7 @@
 
             @pl.when((early >= 0) & (early < 2 * RS_ITEMS))
             def _():
-                arr, g, _, alone = item(early, 1)
+                arr, g, _, alone = item(early, RS_PLAN)
 
                 @pl.when(alone)
                 def _():
@@ -460,7 +486,7 @@
 
             @pl.when((n >= 0) & (n < 2 * RS_ITEMS))
             def _():
-                arr, g, y2, alone = item(n, 1)
+                arr, g, y2, alone = item(n, RS_PLAN)
                 from_up, from_down, to_up, to_down, sink, local = rs_flags(rb, g, y2)
                 c_up, c_down, c_fin = rs_copies(b, arr, g, y2)
 
@@ -536,21 +562,22 @@
         at(6 + b, prep_wot, b)
         at(8 + b, prep_s, 4 * b, 4 * b + 4)
     at(5, merge_z)
-    pair_a = AG_ITEMS // 2
+    at(ORIGIN_U, origin_sends, 1)
     for i in range(4):
-        at(FILL + pair_a * (i // 2 + 1) + EXTRA, norm_part, i)
-        at(FILL + pair_a * (i // 2 + 3) + EXTRA, up_part, i)
+        at(done(0, i), norm_part, i)
+        at(done(1, i), up_part, i)
         for arr in range(2):
-            at(RS_START + RS_ITEMS * arr - 1 + BACK[i], back_part, arr, i)
+            at(RS_START + RS_ITEMS * arr - 1 + BACK[arr][i], back_part, arr, i)
     for slot in range(2):
-        at(FILL + pair_a * (slot + 1) + LATE, finish_h, slot)
-        at(FILL + pair_a * (slot + 3) + LATE, finish_g, slot)
+        last = (2 * slot, 2 * slot + 1) if SLOTS else range(4)
+        at(max(done(0, i) for i in last) + LATE, finish_h, slot)
+        at(max(done(1, i) for i in last) + LATE, finish_g, slot)
     at(GRAD_OUT, grad_out_sent)
-    at(RS_END - 4, grad_out_own)
-    at(FILL + 2 * AG_ITEMS + LATE + 2, small_1)
-    at(FILL + 2 * AG_ITEMS + LATE + 4, small_2)
+    at(RS_END - OWN, grad_out_own)
+    at(max(done(1, 2), done(1, 3)) + LATE + 2, small_1)
+    at(max(done(1, 2), done(1, 3)) + LATE + 4, small_2)
     at(GRAD_IN, grad_in_sent)
-    at(RS_END - 3, grad_in_own)
+    at(RS_END - OWN + 1, grad_in_own)
 
     def both(s, _):
         ag_step(s)
@@ -565,12 +592,12 @@
         rs_step(s - RS_START)
         return 0
 
-    marks = sorted(set(turns) | {0, RS_START, AG_END, RS_END})
+    marks = sorted(set(turns) | {0, RS_START - 2, AG_END, RS_END})
     for lo, hi in zip(marks, marks[1:] + [RS_END]):
         for run in turns.get(lo, ()):
             run()
         if lo < hi:
-            lax.fori_loop(lo, hi, first if lo < RS_START else both if lo < AG_END else second, 0)
+            lax.fori_loop(lo, hi, first if lo < RS_START - 2 else both if lo < AG_END else second, 0)
 
     outs = ((gi_own, gi_ref), (go_own, go_ref), (out_own, out_ref), (gt_own, gt_ref))
 
@@ -584,7 +611,7 @@
     gi_own[...] += gr[0].astype(F32)
     put(0).start()
 
-    alone = (from_xs == 1) | (from_xs == 2) if RS_ALONE else from_xs < 0
+    alone = own_only(RS_PLAN, from_xs, lax.rem(xs, 2))
 
     def fin_wait(arr):
         @pl.when(alone)
@@ -620,7 +647,7 @@
 
     for arr in range(2):
         pl.when(xs != q)(origin(arr, 0).wait_send)
-        pl.when(jnp.logical_not(own_only(from_xs)))(origin(arr, 1).wait_send)
+        pl.when(crosses)(origin(arr, 1).wait_send)
         for k in range(1, 4):
             hg_copy(arr, k).wait_send()
             p_copy(arr, k).wait_send()
@@ -634,7 +661,7 @@
         for b in range(2):
             rb, _ = place(b)
             up, down, _, alone, c_up, c_down, c_y, c_sib = ag_copies(b, rb, n)
-            arr, g, _, _ = item(n, 0)
+            arr, g, _, _ = item(n, AG_PLAN)
             pl.when(up)(c_up.wait_send)
             pl.when(down)(c_down.wait_send)
             c_sib.wait_send()
@@ -649,7 +676,7 @@
     def drain_rs(n, _):
         for b in range(2):
             rb, _ = place(b)
-            arr, g, y2, alone = item(n, 1)
+            arr, g, y2, alone = item(n, RS_PLAN)
             _, _, to_up, to_down, sink, local = rs_flags(rb, g, y2)
             c_up, c_down, c_fin = rs_copies(b, arr, g, y2)
             pl.when(to_up)(c_up.wait_send)

time: 137 us -> 130 us (0.949); the launches traced: 137 us -> 128 us
  Pallas kernels: 137 us -> 127 us
    pallas_call x1, Pallas kernels: 134 us -> 124 us  [body(): pl.pallas_call(kernel, out_shape=shapes, in_specs=[vmem, vmem, vmem, hbm,...]
where the time goes in v3:
time: 130 us; the launch traced here: 128 us
  Pallas kernels  127 us (98%)
    pallas_call x1, Pallas kernels, body(): pl.pallas_call(kernel, out_shape=shapes, in_specs=[vmem, vmem, vmem, hbm,...  124 us
    pallas_call x1, Pallas kernels, body(): pl.pallas_call(finish, out_shape=shapes, in_specs=[hbm] * 4, out_specs=(h...  2.63 us

profile of v3, /device:TPU:10, one launch (start us, length us, event | category | flops | bytes accessed | tf_op | source)
XLA Modules:
  0.0 127.6 jit_solution(8291225753711796944)
XLA Ops:
  0.6 124.2 %block.1 = (bf16[192,256]{1,0:T(8,128)(2,1)}, bf16[192,256]{1,0:T(8,128)(2,1)}, f32[768,384]{1,0:T(8,128)}, f32[384,768]{1,0:T(8,128)}) custom-call(bf16[192,256]{1,0:T(8,128)(2,1)} %bitcast.4, bf16[192,256]{1,0:T(8,128)(2,1)} %bitcast.5, f32[6144]{0:T(1024)} %gain_ref.1, bf16[6144,384]{1,0:T(8,128)(2,1)} %w_in_ref.1, bf16[384,6144]{1,0:T(8,128)(2,1)} %w_out_ref.1), custom_call_target="tpu_custom_call" | custom-call | tf_op jit(solution)/shard_map/block/pallas_call | solution.py:806
  124.8 2.6 %finish.1 = (bf16[192,256]{1,0:T(8,128)(2,1)}, bf16[192,256]{1,0:T(8,128)(2,1)}, f32[768,384]{1,0:T(8,128)}, f32[384,768]{1,0:T(8,128)}) custom-call(bf16[192,256]{1,0:T(8,128)(2,1)} %get-tuple-element.12.refs_0_, bf16[192,256]{1,0:T(8,128)(2,1)} %get-tuple-element.13.refs_1_, f32[768,384]{1,0:T(8,128)} %get-tuple-element.14.refs_2_, ...), custom_call_target="tpu_custom_call" | custom-call | tf_op jit(solution)/shard_map/finish/pallas_call | solution.py:817

commit v4 on v3

--- a/solution.py
+++ b/solution.py
@@ -611,6 +611,57 @@
     gi_own[...] += gr[0].astype(F32)
     put(0).start()
 
+    for arr in range(2):
+        pl.when(xs != q)(origin(arr, 0).wait_send)
+        pl.when(crosses)(origin(arr, 1).wait_send)
+        for k in range(1, 4):
+            hg_copy(arr, k).wait_send()
+            p_copy(arr, k).wait_send()
+    for i in range(2):
+        gr_copy(i).wait_send()
+        sm_copy(i).wait_send()
+    for k in range(1, 8):
+        smz_copy(k).wait_send()
+
+    def drain_ag(n, _):
+        for b in range(2):
+            rb, _ = place(b)
+            up, down, _, alone, c_up, c_down, c_y, c_sib = ag_copies(b, rb, n)
+            arr, g, _, _ = item(n, AG_PLAN)
+            pl.when(up)(c_up.wait_send)
+            pl.when(down)(c_down.wait_send)
+            c_sib.wait_send()
+
+            @pl.when(alone)
+            def _():
+                c_y.wait_send()
+                sib_copy(arr, g, b, 1 - yl, c).wait_send()
+
+        return 0
+
+    def drain_rs(n, _):
+        for b in range(2):
+            rb, _ = place(b)
+            arr, g, y2, alone = item(n, RS_PLAN)
+            _, _, to_up, to_down, sink, local = rs_flags(rb, g, y2)
+            c_up, c_down, c_fin = rs_copies(b, arr, g, y2)
+            pl.when(to_up)(c_up.wait_send)
+            pl.when(to_down)(c_down.wait_send)
+            pl.when(sink & jnp.logical_not(local))(c_fin.wait_send)
+            pl.when(alone)(ry_copy(arr, g, b).wait_send)
+            pl.when((y2 == 0) | alone)(b_copy(arr, g, b).wait_send)
+        return 0
+
+    lax.fori_loop(0, 2 * AG_ITEMS, drain_ag, 0)
+    lax.fori_loop(0, 2 * RS_ITEMS, drain_rs, 0)
+
+    for k in range(1, 8):
+        stz_copy(k).wait_send()
+    for k in range(1, 4):
+        stx_copy(k).wait_send()
+    for i in range(2):
+        st_copy(i).wait_send()
+
     alone = own_only(RS_PLAN, from_xs, lax.rem(xs, 2))
 
     def fin_wait(arr):
@@ -645,56 +696,6 @@
 
     put(3).start()
 
-    for arr in range(2):
-        pl.when(xs != q)(origin(arr, 0).wait_send)
-        pl.when(crosses)(origin(arr, 1).wait_send)
-        for k in range(1, 4):
-            hg_copy(arr, k).wait_send()
-            p_copy(arr, k).wait_send()
-    for i in range(2):
-        gr_copy(i).wait_send()
-        sm_copy(i).wait_send()
-    for k in range(1, 8):
-        smz_copy(k).wait_send()
-
-    def drain_ag(n, _):
-        for b in range(2):
-            rb, _ = place(b)
-            up, down, _, alone, c_up, c_down, c_y, c_sib = ag_copies(b, rb, n)
-            arr, g, _, _ = item(n, AG_PLAN)
-            pl.when(up)(c_up.wait_send)
-            pl.when(down)(c_down.wait_send)
-            c_sib.wait_send()
-
-            @pl.when(alone)
-            def _():
-                c_y.wait_send()
-                sib_copy(arr, g, b, 1 - yl, c).wait_send()
-
-        return 0
-
-    def drain_rs(n, _):
-        for b in range(2):
-            rb, _ = place(b)
-            arr, g, y2, alone = item(n, RS_PLAN)
-            _, _, to_up, to_down, sink, local = rs_flags(rb, g, y2)
-            c_up, c_down, c_fin = rs_copies(b, arr, g, y2)
-            pl.when(to_up)(c_up.wait_send)
-            pl.when(to_down)(c_down.wait_send)
-            pl.when(sink & jnp.logical_not(local))(c_fin.wait_send)
-            pl.when(alone)(ry_copy(arr, g, b).wait_send)
-            pl.when((y2 == 0) | alone)(b_copy(arr, g, b).wait_send)
-        return 0
-
-    lax.fori_loop(0, 2 * AG_ITEMS, drain_ag, 0)
-    lax.fori_loop(0, 2 * RS_ITEMS, drain_rs, 0)
-
-    for k in range(1, 8):
-        stz_copy(k).wait_send()
-    for k in range(1, 4):
-        stx_copy(k).wait_send()
-    for i in range(2):
-        st_copy(i).wait_send()
     for i in range(4):
         put(i).wait()
 

time: 130 us -> 129 us (level)
  no operation moved by 1% of the time
where the time goes in v4:
time: 129 us; the launch traced here: 127 us
  Pallas kernels  126 us (98%)
    pallas_call x1, Pallas kernels, body(): pl.pallas_call(kernel, out_shape=shapes, in_specs=[vmem, vmem, vmem, hbm,...  123 us
    pallas_call x1, Pallas kernels, body(): pl.pallas_call(finish, out_shape=shapes, in_specs=[hbm] * 4, out_specs=(h...  2.63 us

profile of v4, /device:TPU:10, one launch (start us, length us, event | category | flops | bytes accessed | tf_op | source)
XLA Modules:
  0.0 126.9 jit_solution(13300432023849456478)
XLA Ops:
  0.6 123.4 %block.1 = (bf16[192,256]{1,0:T(8,128)(2,1)}, bf16[192,256]{1,0:T(8,128)(2,1)}, f32[768,384]{1,0:T(8,128)}, f32[384,768]{1,0:T(8,128)}) custom-call(bf16[192,256]{1,0:T(8,128)(2,1)} %bitcast.4, bf16[192,256]{1,0:T(8,128)(2,1)} %bitcast.5, f32[6144]{0:T(1024)} %gain_ref.1, bf16[6144,384]{1,0:T(8,128)(2,1)} %w_in_ref.1, bf16[384,6144]{1,0:T(8,128)(2,1)} %w_out_ref.1), custom_call_target="tpu_custom_call" | custom-call | tf_op jit(solution)/shard_map/block/pallas_call | solution.py:807
  124.1 2.6 %finish.1 = (bf16[192,256]{1,0:T(8,128)(2,1)}, bf16[192,256]{1,0:T(8,128)(2,1)}, f32[768,384]{1,0:T(8,128)}, f32[384,768]{1,0:T(8,128)}) custom-call(bf16[192,256]{1,0:T(8,128)(2,1)} %get-tuple-element.12.refs_0_, bf16[192,256]{1,0:T(8,128)(2,1)} %get-tuple-element.13.refs_1_, f32[768,384]{1,0:T(8,128)} %get-tuple-element.14.refs_2_, ...), custom_call_target="tpu_custom_call" | custom-call | tf_op jit(solution)/shard_map/finish/pallas_call | solution.py:818
